TPU v7x, 32 devices: a whole 2x2x4 slice. The times are simulated.
32 devices in a mesh: groups: 2 (over y), seq: 16 (over z, x, core).
Axes of the slice: x: 2, y: 2, z: 4, core: 2. Of those that a mesh axis runs over, the one named last changes fastest.
Arguments:
- queries: bfloat16 [4096, 4096], P(('groups', 'seq')), parts along dimension 0, may hold values from -6 to 6
- keys: bfloat16 [4096, 4096], P(('groups', 'seq')), parts along dimension 0, may hold values from -6 to 6
- values: bfloat16 [4096, 4096], P(('groups', 'seq')), parts along dimension 0, may hold values from -6 to 6
- kept: int32 [64, 4, 8], P('groups'), parts along dimension 0, may hold values from 0 to 15, as said below
- counts: int32 [64, 4], P('groups'), parts along dimension 0, may hold values from 4 to 8
Outputs:
- attended: bfloat16 [4096, 4096], P(('groups', 'seq')), parts along dimension 0
There are 2 independent parts, one for each index of `groups`. A program takes and returns all parts, laid end to end along the dimension named above; each array names one. Nothing has to cross between parts.
Inputs may be any that keep to these rules, and one draw needn't show every extreme that they name: `kept`: for head h and query tile t, slots 0 to 3 hold the key tiles 4 * t to 4 * t + 3 in order; the entries of one list are distinct; slots at or past counts[h, t] are padding.
All inputs are finite; a program needn't handle non-finite values.
Results may differ from a plain program's by a relative error of at most 0.0046.
Values may be sent and summed in bfloat16 or wider, within the bound.
No kernel may reach another device: no remote copies, remote signals or barrier semaphores. Data moves between devices by JAX's collectives and lax.ppermute only.
A program may use at most 128 MiB of HBM per device.

v0:
```python
import functools

import jax
import jax.numpy as jnp
from jax import lax
from jax.experimental import pallas as pl
from jax.experimental.pallas import tpu as pltpu
from jax.sharding import PartitionSpec as P

HEAD_DIM = 128
QTILE = 512
KTILE = 128
GROUP = 4
OWN = QTILE // KTILE
SIZES = ((5, 16), (6, 18), (7, 20))
MIB = 1 << 20
SMEM = pl.BlockSpec(memory_space=pltpu.SMEM)
VMEM = pl.BlockSpec(memory_space=pltpu.VMEM)
HBM = pl.BlockSpec(memory_space=pl.ANY)


def params(mib):
    return pltpu.CompilerParams(vmem_limit_bytes=mib * MIB)


def cost(flops):
    return pl.CostEstimate(flops=flops, bytes_accessed=8 << 20, transcendentals=0)


def thirds(late):
    return late // 3, late // 3, late - 2 * (late // 3)


def columns(head):
    if isinstance(head, int):
        return pl.ds(head * HEAD_DIM, HEAD_DIM)
    return pl.ds(pl.multiple_of(head * HEAD_DIM, HEAD_DIM), HEAD_DIM)


def dot(a, b):
    return jnp.dot(a, b, preferred_element_type=jnp.float32)


def lists_kernel(planes, slots, where, kept, counts, sends, takes, choice):
    plane, pair = where[0], where[1] >> 1
    heads = kept.shape[1]
    shape = (planes * OWN, heads)
    half = (planes * OWN // 2, heads)
    ids = lax.broadcasted_iota(jnp.int32, shape, 0)
    chips = lax.broadcasted_iota(jnp.int32, half, 0)
    bit = jnp.left_shift(jnp.int32(1), lax.broadcasted_iota(jnp.int32, shape, 1))
    lane = lax.broadcasted_iota(jnp.int32, (1, HEAD_DIM), 1)
    most = jnp.zeros((planes * OWN // 2, 1), jnp.int32)
    touched = jnp.zeros((1, 1), jnp.int32)
    taken = jnp.zeros(shape, jnp.int32)
    wanted = []
    for t in range(planes):
        hits = jnp.zeros(shape, jnp.int32)
        per_chip = jnp.zeros(half, jnp.int32)
        for j in range(OWN, slots):
            tile = kept[t * slots + j : t * slots + j + 1, :]
            live = counts[t : t + 1, :] > j
            hits = jnp.where((ids == tile) & live, 1, hits)
            per_chip = per_chip + jnp.where((chips == (tile >> 1)) & live, 1, 0)
        most = jnp.maximum(most, jnp.sum(per_chip, axis=1, keepdims=True))
        for side in range(2):
            some = jnp.max(jnp.where(((ids >> 1) & 1) == side, hits, 0), axis=0, keepdims=True)
            touched = jnp.maximum(touched, jnp.sum(some, axis=1, keepdims=True))
        bits = hits * bit
        for turn in range(2):
            wanted.append(jnp.sum(jnp.where(ids == 2 * pair + turn, hits, 0), axis=0, keepdims=True))
        taken = jnp.where(plane == t, bits, taken)
    square = (heads, heads)
    at, head = lax.broadcasted_iota(jnp.int32, square, 0), lax.broadcasted_iota(jnp.int32, square, 1)
    before = jnp.where(at < head, 1.0, 0.0)
    named = jnp.concatenate(wanted, axis=0)
    rank = dot(named.astype(jnp.float32), before).astype(jnp.int32)
    rows = jnp.zeros((heads, HEAD_DIM), jnp.int32)
    count = jnp.zeros((1, HEAD_DIM), jnp.int32)
    for i in range(2 * planes):
        here = (at == rank[i : i + 1, :]) & (named[i : i + 1, :] == 1)
        rows = jnp.where(lane == i, jnp.sum(jnp.where(here, head, 0), axis=1, keepdims=True), rows)
        count = jnp.where(lane == i, jnp.sum(named[i : i + 1, :], axis=1, keepdims=True), count)
    sends[0:heads, :] = rows
    sends[heads : heads + 8, :] = jnp.broadcast_to(count, (8, HEAD_DIM))
    takes[...] = jnp.where(
        lane == 0,
        jnp.sum(taken, axis=1, keepdims=True),
        jnp.sum(jnp.where(taken != 0, 1, 0), axis=1, keepdims=True),
    )
    top, wide = jnp.max(most), jnp.max(touched)
    index = jnp.int32(len(SIZES))
    for i, (room, late) in reversed(list(enumerate(SIZES))):
        index = jnp.where((top <= 2 * room) & (wide <= late), i, index)
    choice[0] = index


def pack_kernel(heads, planes, room, where, sends, k_ref, v_ref, mate_k, mate_v, *outs):
    plane, core = where[0], where[3]
    for step, out in enumerate(outs, 1):
        lane = 2 * lax.rem(plane + step, planes)
        first, both = sends[heads, lane], sends[heads, lane] + sends[heads, lane + 1]

        def take(slot, carry, out=out, lane=lane, first=first):
            at = core * room + slot
            turn = jnp.where(at >= first, 1, 0)
            head = sends[at - turn * first, lane + turn]

            @pl.when(core == turn)
            def _():
                out[slot, 0] = k_ref[:, columns(head)].T
                out[slot, 1] = v_ref[:, columns(head)]

            @pl.when(core != turn)
            def _():
                out[slot, 0] = mate_k[:, columns(head)].T
                out[slot, 1] = mate_v[:, columns(head)]

            return carry

        lax.fori_loop(0, jnp.clip(both - core * room, 0, room), take, 0)


def plan_kernel(heads, planes, room, where, takes, pair, begin, order, far):
    plane, side, core = where[0], where[2], where[3]
    near, other, starts = [], [], []
    for step in range(1, planes):
        source = lax.rem(plane - step + planes, planes) * OWN
        for turn in range(2):
            near.append(takes[source + 2 * side + turn, 0])
            starts.append(takes[source + 2 * side, 1] if turn else jnp.int32(0))
            other.append(takes[source + 2 * (1 - side) + turn, 0])
    any_near = functools.reduce(jnp.bitwise_or, near)
    any_other = functools.reduce(jnp.bitwise_or, other)

    def held(bits):
        return lax.fori_loop(0, heads, lambda h, n: n + ((bits >> h) & 1), jnp.int32(0))

    def put(head, state):
        a, b, c, d, pairs, *used = state
        none, far_none = 1 - ((any_near >> head) & 1), 1 - ((any_other >> head) & 1)
        at = jnp.where(none == 1, a, b)
        order[at] = head
        far[jnp.where(far_none == 1, c, d)] = head
        begin[head] = pairs
        for i, bits in enumerate(near):
            hit = (bits >> head) & 1
            sender = jnp.where(used[i] >= room, 1, 0)
            box = i // 2 * 2 + jnp.where(sender == core, 0, 1)

            @pl.when(hit == 1)
            def _(i=i, pairs=pairs, used=used, sender=sender, box=box):
                pair[pairs] = head * 4096 + box * room + used[i] - sender * room

            pairs = pairs + hit
            used = used[:i] + [used[i] + hit] + used[i + 1 :]
        return (a + none, b + 1 - none, c + far_none, d + 1 - far_none, pairs, *used)

    zero = jnp.int32(0)
    first = (zero, heads - held(any_near), zero, heads - held(any_other), zero, *starts)
    begin[heads] = lax.fori_loop(0, heads, put, first)[4]


def soften(q, k_t, v):
    s = dot(q, k_t) * (1.0 / HEAD_DIM**0.5)
    m = jnp.max(s, axis=1, keepdims=True)
    w = jnp.exp(s - m)
    l = jnp.sum(w, axis=1, keepdims=True)
    return dot(w.astype(jnp.bfloat16), v) / l, m + jnp.log(l)


def here_kernel(heads, q_ref, k_ref, v_ref, mate_k, mate_v, out, lse_out, turned):
    lane = lax.broadcasted_iota(jnp.int32, lse_out.shape, 1)

    def attend(head, lse):
        at = columns(head)
        k_t = jnp.concatenate([k_ref[:, at].T, mate_k[:, at].T], axis=1)
        turned[head] = k_t
        v = jnp.concatenate([v_ref[:, at], mate_v[:, at]], axis=0)
        o, new = soften(q_ref[:, at], k_t, v)
        out[head] = o
        return jnp.where(lane == head, new, lse)

    lse_out[...] = lax.fori_loop(0, heads, attend, jnp.zeros(lse_out.shape, jnp.float32), unroll=4)


def far_kernel(start, order, lse_ref, q_ref, turned, v_ref, mate_v, *outs):
    *parts, lse_out = outs
    lane = lax.broadcasted_iota(jnp.int32, lse_out.shape, 1)
    lse = lse_ref[...]
    for part in parts:

        def attend(i, lse, part=part, start=start):
            head = order[start + i]
            at = columns(head)
            v = jnp.concatenate([v_ref[:, at], mate_v[:, at]], axis=0)
            o, new = soften(q_ref[:, at], turned[head], v)
            part[i] = o.astype(part.dtype)
            return jnp.where(lane == head, new, lse)

        lse = lax.fori_loop(0, part.shape[0], attend, lse, unroll=4)
        start += part.shape[0]
    lse_out[...] = lse


def late_kernel(sends, early, by_head, room, order, pair, begin, q_ref, o_ref, lse_ref, *rest):
    boxes, rest = rest[: sends], rest[sends:]
    *outs, lse_out, tiles, partial, level, sems = rest
    copies = [
        pltpu.make_async_copy(box, tiles.at[pl.ds(b * room, room)], sems.at[b]) for b, box in enumerate(boxes)
    ]
    for copy in copies:
        copy.start()
    heads = order.shape[0]
    shape = lse_ref.shape
    most = partial.shape[0]
    lane = lax.broadcasted_iota(jnp.int32, shape, 1)
    total = begin[heads]
    for copy in copies:
        copy.wait()

    if by_head:
        outs[0][...] = o_ref[...]
    wide = not by_head and heads - early <= 18
    width = 8 if wide else 4

    def several(i, carry):
        for j in range(width):
            at = jnp.minimum(width * i + j, total - 1)
            code = pair[at]
            head, tile = code >> 12, code & 4095
            o, new = soften(q_ref[:, columns(head)], tiles[tile, 0], tiles[tile, 1])
            partial[at] = o
            level[at] = jnp.broadcast_to(new, shape)
        return carry

    lax.fori_loop(0, lax.div(total + width - 1, width), several, 0)

    def join(i, lse, out, skip):
        head = order[early + skip + i]
        start, end = begin[head], begin[head + 1]
        base = jnp.sum(jnp.where(lane == head, lse_ref[...], 0.0), axis=1, keepdims=True)
        base = jnp.broadcast_to(base, shape)
        spots = [jnp.minimum(start + e, most - 1) for e in range(4)]
        levels = [jnp.where(start + e < end, level[p], -1e30) for e, p in enumerate(spots)]
        m = functools.reduce(jnp.maximum, levels, base)
        l = jnp.exp(base - m)
        o = l * o_ref[head if by_head else skip + i]
        for e, p in enumerate(spots):
            w = jnp.exp(levels[e] - m)
            l = l + w
            o = o + jnp.where(start + e < end, w * partial[p], 0.0)
        out[head if by_head else i] = (o / l).astype(out.dtype)
        return jnp.where(lane == head, m + jnp.log(l), lse)

    lse, skip = lse_ref[...], 0
    for out in outs:
        count = heads - early if by_head else out.shape[0]
        unroll = count if wide else 2
        lse = lax.fori_loop(0, count, functools.partial(join, out=out, skip=skip), lse, unroll=unroll)
        skip += out.shape[0]
    lse_out[...] = lse if by_head else lse.T[:heads]


def merge_kernel(far, mine, lse_here, lse_got, *rest):
    *got, result, out, sems = rest
    a, b = lse_here[...], lse_got[...]
    heads = b.shape[0]
    b = jnp.concatenate([b, jnp.zeros((a.shape[1] - heads, a.shape[0]), b.dtype)], axis=0).T
    m = jnp.maximum(a, b)
    wa, wb = jnp.exp(a - m), jnp.exp(b - m)
    share = wb / (wa + wb)
    lane = lax.broadcasted_iota(jnp.int32, a.shape, 1)
    leaving = []
    for part in got:
        for i in range(part.shape[0]):
            slot = len(leaving)
            head = far[slot]
            at = columns(head)
            weight = jnp.sum(jnp.where(lane == head, share, 0.0), axis=1, keepdims=True)
            own = mine[head]
            out[:, at] = (own + weight * (part[i].astype(jnp.float32) - own)).astype(out.dtype)
            leaving.append(pltpu.make_async_copy(out.at[:, at], result.at[:, at], sems.at[slot]))
            leaving[-1].start()
    for copy in leaving:
        copy.wait()


def exchange(room, late, planes, queries, keys, values, mate_k, sends, takes, where):
    rows, features = queries.shape
    heads = features // HEAD_DIM
    early = heads - late
    f32, bf16, i32 = jnp.float32, jnp.bfloat16, jnp.int32
    shape = jax.ShapeDtypeStruct
    tile = (rows, HEAD_DIM)
    count = planes * OWN
    across = [(d, d ^ 2) for d in range(count)]
    beside = [(d, d ^ 1) for d in range(count)]
    barrier = lax.optimization_barrier

    mate_v = lax.ppermute(values, "seq", beside)
    far_q = lax.ppermute(queries, "seq", across)
    packed = pl.pallas_call(
        functools.partial(pack_kernel, heads, planes, room),
        out_shape=[shape((room, 2) + tile, bf16)] * (planes - 1),
        in_specs=[SMEM] * 2 + [VMEM] * 4,
        out_specs=[VMEM] * (planes - 1),
        compiler_params=params(8 + room // 4),
        cost_estimate=cost(4 << 30),
        name="pack",
    )(where, sends, keys, values, mate_k, mate_v)
    landed = [
        lax.ppermute(packed[step - 1], "seq", [(d, (d + OWN * step) % count) for d in range(count)])
        for step in range(1, planes)
    ]

    where, takes, *packed = barrier((where, takes, *packed))
    most_pairs = min(4 * (planes - 1) * room, HEAD_DIM)
    pair, begin, order, far = pl.pallas_call(
        functools.partial(plan_kernel, heads, planes, room),
        out_shape=[shape((n,), i32) for n in (most_pairs, heads + 1, heads, heads)],
        in_specs=[SMEM] * 2,
        out_specs=[SMEM] * 4,
        compiler_params=params(4),
        cost_estimate=cost(4 << 30),
        name="plan",
    )(where, takes)
    here, lse_here, turned = pl.pallas_call(
        functools.partial(here_kernel, heads),
        out_shape=[shape((heads,) + tile, f32), shape(tile, f32), shape((heads, HEAD_DIM, 2 * rows), bf16)],
        in_specs=[VMEM] * 5,
        out_specs=[VMEM] * 3,
        compiler_params=params(14),
        cost_estimate=cost(1 << 30),
        name="here",
    )(queries, keys, values, mate_k, mate_v)

    def attend_far(order, lse, start, parts):
        return pl.pallas_call(
            functools.partial(far_kernel, start),
            out_shape=[shape((n,) + tile, kind) for n, kind in parts] + [shape(tile, f32)],
            in_specs=[SMEM] + [VMEM] * 5,
            out_specs=[VMEM] * (len(parts) + 1),
            compiler_params=params(12),
            cost_estimate=cost(1 << 30),
            name="far",
        )(order, lse, far_q, turned, values, mate_v)

    second = min(early, thirds(late)[-1] + 1)
    parts = [n for n in (early - second, second) if n]
    lse_far, arrived = lse_here, []
    if early:
        sent, lse_far = attend_far(order, lse_far, 0, [(parts[0], bf16)])
        arrived = [lax.ppermute(sent, "seq", across)]
    kinds = [(n, bf16) for n in parts[1:]] + [(late, f32)]
    *sent, rest, lse_far = attend_far(order, lse_far, early - sum(parts[1:]), kinds)
    arrived += [lax.ppermute(x, "seq", across) for x in sent]
    *landed, rest, lse_far, first = barrier((*landed, rest, lse_far, arrived[:-1]))
    arrived = first + arrived[len(first) :]
    boxes = []
    for got in landed:
        boxes += [got, lax.ppermute(got, "seq", beside)]

    def add_extras(q, o, lse, by_head, parts):
        return pl.pallas_call(
            functools.partial(late_kernel, len(boxes), early, by_head, room),
            out_shape=[shape((n,) + tile, kind) for n, kind in parts] + [shape(tile if by_head else (heads, rows), f32)],
            in_specs=[SMEM] * 3 + [VMEM] * 3 + [HBM] * len(boxes),
            out_specs=[VMEM] * (len(parts) + 1),
            scratch_shapes=[
                pltpu.VMEM((len(boxes) * room, 2) + tile, bf16),
                pltpu.VMEM((most_pairs,) + tile, f32),
                pltpu.VMEM((most_pairs,) + tile, f32),
                pltpu.SemaphoreType.DMA((len(boxes),)),
            ],
            compiler_params=params(min(8 + 2 * room, 48)),
            cost_estimate=cost(1 << 20),
            name="late",
        )(order, pair, begin, q, o, lse, *boxes)

    *far_late, lse_far = add_extras(far_q, rest, lse_far, False, [(n, bf16) for n in thirds(late)])
    arrived = [lax.ppermute(lse_far, "seq", across), *arrived] + [lax.ppermute(x, "seq", across) for x in far_late]
    here, lse_here = add_extras(queries, here, lse_here, True, [(heads, f32)])

    return pl.pallas_call(
        merge_kernel,
        out_shape=pltpu.HBM((rows, features), bf16),
        in_specs=[SMEM] + [VMEM] * (2 + len(arrived)),
        out_specs=pl.BlockSpec(memory_space=pltpu.HBM),
        scratch_shapes=[
            pltpu.VMEM((rows, features), bf16),
            pltpu.SemaphoreType.DMA((heads,)),
        ],
        compiler_params=params(12),
        cost_estimate=cost(1 << 20),
        name="merge",
    )(far, here, lse_here, *arrived)


def per_plane(queries, keys, values, kept, counts):
    heads, planes, slots = kept.shape
    device = lax.axis_index("seq").astype(jnp.int32)
    where = jnp.stack([device >> 2, device, (device >> 1) & 1, device & 1])
    beside = [(d, d ^ 1) for d in range(planes * OWN)]
    mate_k = lax.ppermute(keys, "seq", beside)
    shape = jax.ShapeDtypeStruct
    sends, takes, choice = pl.pallas_call(
        functools.partial(lists_kernel, planes, slots),
        out_shape=[
            shape((heads + 8, HEAD_DIM), jnp.int32),
            shape((planes * OWN, HEAD_DIM), jnp.int32),
            shape((1,), jnp.int32),
        ],
        in_specs=[SMEM] + [VMEM] * 2,
        out_specs=[VMEM] * 2 + [SMEM],
        compiler_params=params(60),
        name="lists",
    )(where, kept.transpose(1, 2, 0).reshape(planes * slots, heads), counts.T)
    sizes = SIZES + ((heads, heads),)
    return lax.switch(
        choice[0],
        [functools.partial(exchange, room, late, planes) for room, late in sizes],
        queries,
        keys,
        values,
        mate_k,
        sends,
        takes,
        where,
    )


def attend_tile(query_tile, key_tiles, value_tiles, slot_list, live_count):
    row_count = query_tile.shape[0]
    factor = 1.0 / query_tile.shape[1] ** 0.5
    start_state = (
        jnp.full((row_count,), -1e30, jnp.float32),
        jnp.zeros((row_count,), jnp.float32),
        jnp.zeros((row_count, query_tile.shape[1]), jnp.float32),
    )

    def advance(block_num, state_now):
        running, totals, numerator = state_now
        first = (block_num * GROUP).astype(jnp.int32)
        chosen = lax.dynamic_slice_in_dim(slot_list, first, GROUP)
        key_block = key_tiles[chosen].reshape(GROUP * KTILE, query_tile.shape[1])
        value_block = value_tiles[chosen].reshape(GROUP * KTILE, query_tile.shape[1])
        scores = jnp.dot(query_tile, key_block.T, preferred_element_type=jnp.float32) * factor
        live_mask = jnp.repeat(first + jnp.arange(GROUP, dtype=jnp.int32) < live_count, KTILE)
        scores = jnp.where(live_mask[None, :], scores, -1e30)
        new_max = jnp.maximum(running, jnp.max(scores, axis=1))
        rescale = jnp.exp(running - new_max)
        weights = jnp.exp(scores - new_max[:, None])
        totals = totals * rescale + jnp.sum(weights, axis=1)
        numerator = numerator * rescale[:, None] + jnp.dot(
            weights.astype(jnp.bfloat16), value_block, preferred_element_type=jnp.float32
        )
        return (new_max, totals, numerator)

    block_total = (live_count + GROUP - 1) // GROUP
    running, totals, numerator = lax.fori_loop(jnp.int32(0), block_total, advance, start_state)
    return (numerator / totals[:, None]).astype(jnp.bfloat16)


def per_device(queries, keys, values, kept, counts):
    local_rows, feature_count = queries.shape
    shards = lax.axis_size("seq")
    device = lax.axis_index("seq")
    head_count = feature_count // HEAD_DIM
    replicas = max(1, shards // head_count)
    slots_here = max(1, head_count // shards)
    total_rows = local_rows * shards
    tile_count = counts.shape[1]
    stacked = jnp.stack([queries, keys, values])
    copied = jnp.broadcast_to(
        stacked.reshape(3, local_rows, head_count, 1, HEAD_DIM),
        (3, local_rows, head_count, replicas, HEAD_DIM),
    )
    copied = copied.reshape(3, local_rows, head_count * replicas, HEAD_DIM)
    arrived = lax.all_to_all(copied, "seq", split_axis=2, concat_axis=1, tiled=True)
    head_data = arrived.transpose(2, 0, 1, 3)
    tiles_each = tile_count // replicas
    results = []
    for j in range(slots_here):
        global_slot = device * slots_here + j
        head_id = global_slot // replicas
        replica_id = global_slot % replicas
        slot_rows = lax.dynamic_index_in_dim(kept, head_id, 0, keepdims=False)
        count_row = lax.dynamic_index_in_dim(counts, head_id, 0, keepdims=False)
        all_queries = head_data[j, 0]
        key_tiles = head_data[j, 1].reshape(total_rows // KTILE, KTILE, HEAD_DIM)
        value_tiles = head_data[j, 2].reshape(total_rows // KTILE, KTILE, HEAD_DIM)
        rounds = jnp.arange(tiles_each, dtype=jnp.int32)
        tile_ids = replica_id * tiles_each + rounds

        def process(i, output):
            tile_id = tile_ids[i]
            query_tile = lax.dynamic_slice_in_dim(all_queries, tile_id * QTILE, QTILE, 0)
            finished = attend_tile(
                query_tile, key_tiles, value_tiles, slot_rows[tile_id], count_row[tile_id]
            )
            return lax.dynamic_update_slice_in_dim(output, finished, tile_id * QTILE, 0)

        results.append(
            lax.fori_loop(0, tiles_each, process, jnp.zeros((total_rows, HEAD_DIM), jnp.bfloat16))
        )
    gathered = jnp.stack(results, axis=1)
    returned = lax.all_to_all(gathered, "seq", split_axis=0, concat_axis=1, tiled=True)
    combined = (
        returned.reshape(local_rows, head_count, replicas, HEAD_DIM).astype(jnp.float32).sum(axis=2)
    )
    return combined.astype(jnp.bfloat16).reshape(local_rows, feature_count)


def solution(mesh):
    by_rows = P(("groups", "seq"), None)
    placed = (by_rows, by_rows, by_rows, P("groups", None, None), P("groups", None))

    def step(queries, keys, values, kept, counts):
        heads, planes, slots = kept.shape
        one_tile_each = queries.shape[0] == KTILE and mesh.shape["seq"] == planes * OWN
        fits = heads % 8 == 0 and heads <= 32 and heads * (slots - OWN) <= HEAD_DIM and planes == 4
        run = per_plane if one_tile_each and fits else per_device
        return run(queries, keys, values, kept, counts)

    return jax.shard_map(step, mesh=mesh, in_specs=placed, out_specs=by_rows, check_vma=False)
```

profile of v0, /device:TPU:1, one launch (start us, length us, event | category | flops | bytes accessed | tf_op | source)
XLA Modules:
  0.0 63.2 jit_solution(7481746529449766006)
XLA Ops:
  0.1 1.5 %lists.1 = (s32[40,128]{1,0:T(8,128)S(1)}, s32[16,128]{1,0:T(8,128)S(1)}, s32[1]{0:T(128)}) custom-call(s32[4]{0:T(128)S(1)} %pad_add_fusion.where, s32[32,32]{1,0:T(8,128)} %bitcast.9, s32[4,32]{1,0:T(4,128)} %bitcast.10), custom_call_target="tpu_custom_call" | custom-call | tf_op jit(solution)/shard_map/lists/pallas_call | solution.py:407
  2.2 0.6 collective-permute-done.54
  2.9 60.1 %conditional.1 = (bf16[128,4096]{1,0:T(8,128)(2,1)}) conditional(s32[]{:T(128)} %bitcast.7, (bf16[128,4096]{1,0:T(8,128)(2,1)}, s32[4]{0:T(128)S(1)}, s32[40,128]{1,0:T(8,128)S(1)}, bf16[128,4096]{1,0:T(8,128)(2,1)}, bf16[128,4096]{1,0:T(8,128)(2,1)S(1)}, /*index=5*/s32[16,128]{1,0:T(8,128)S(1)}, ...), branch_computations={%region_0.0_spmd, %region_1.0_spmd, %region_2.0_spmd, %region_3.0_... | conditional | flops 11814305792 | bytes 184615584 | solution.py:420
  3.0 2.6 %collective-permute-start.4 = (bf16[128,4096]{1,0:T(8,128)(2,1)}, bf16[128,4096]{1,0:T(8,128)(2,1)S(1)}, u32[]{:S(2)}, u32[]{:S(2)}) collective-permute-start(bf16[128,4096]{1,0:T(8,128)(2,1)} %get-tuple-element.225.q_ref), channel_id=1, source_target_pairs={{0,2},{1,3},{2,0},{3,1},{4,6},{5,7},{6,4},{7,5},{8,10},{9,11},{10,... | collective-permute-start | bytes 3145736 | tf_op jit(solution)/shard_map/cond/branch_0_fun/ppermute | solution.py:302
  5.8 1.8 %pack.4 = (bf16[5,2,128,128]{3,2,1,0:T(8,128)(2,1)S(1)}, bf16[5,2,128,128]{3,2,1,0:T(8,128)(2,1)S(1)}, bf16[5,2,128,128]{3,2,1,0:T(8,128)(2,1)S(1)}) custom-call(s32[4]{0:T(128)S(1)} %get-tuple-element.75.where, s32[40,128]{1,0:T(8,128)S(1)} %get-tuple-element.68.sends, bf16[128,4096]{1,0:T(8,128)(2,1)} %get-tuple-element.69.k_ref, ...), custom_call_target="tpu_custom_call" | custom-call | flops 4294967296 | bytes 8388608 | tf_op jit(solution)/shard_map/cond/branch_0_fun/pack/pallas_call | solution.py:303
  7.5 2.5 %collective-permute-start.1 = (bf16[5,2,128,128]{3,2,1,0:T(8,128)(2,1)S(1)}, bf16[5,2,128,128]{3,2,1,0:T(8,128)(2,1)S(1)}, u32[]{:S(2)}, u32[]{:S(2)}) collective-permute-start(bf16[5,2,128,128]{3,2,1,0:T(8,128)(2,1)S(1)} %get-tuple-element.72), channel_id=1, source_target_pairs={{0,4},{1,5},{2,6},{3,7},{4,8},{5,9},{6,10},{7,11},{8,12},{9,13},{1... | collective-permute-start | bytes 983048 | tf_op jit(solution)/shard_map/cond/branch_0_fun/ppermute | solution.py:313
  10.0 2.3 %collective-permute-start.2 = (bf16[5,2,128,128]{3,2,1,0:T(8,128)(2,1)S(1)}, bf16[5,2,128,128]{3,2,1,0:T(8,128)(2,1)S(1)}, u32[]{:S(2)}, u32[]{:S(2)}) collective-permute-start(bf16[5,2,128,128]{3,2,1,0:T(8,128)(2,1)S(1)} %get-tuple-element.73), channel_id=1, source_target_pairs={{0,8},{1,9},{2,10},{3,11},{4,12},{5,13},{6,14},{7,15},{8,0},{9,1},... | collective-permute-start | bytes 983048 | tf_op jit(solution)/shard_map/cond/branch_0_fun/ppermute | solution.py:313
  12.3 1.1 %collective-permute-start.3 = (bf16[5,2,128,128]{3,2,1,0:T(8,128)(2,1)S(1)}, bf16[5,2,128,128]{3,2,1,0:T(8,128)(2,1)S(1)}, u32[]{:S(2)}, u32[]{:S(2)}) collective-permute-start(bf16[5,2,128,128]{3,2,1,0:T(8,128)(2,1)S(1)} %get-tuple-element.74), channel_id=1, source_target_pairs={{0,12},{1,13},{2,14},{3,15},{4,0},{5,1},{6,2},{7,3},{8,4},{9,5},{1... | collective-permute-start | bytes 983048 | tf_op jit(solution)/shard_map/cond/branch_0_fun/ppermute | solution.py:313
  13.4 4.3 %here.4 = (f32[32,128,128]{2,1,0:T(8,128)S(1)}, f32[128,128]{1,0:T(8,128)S(1)}, bf16[32,128,256]{2,1,0:T(8,128)(2,1)S(1)}) custom-call(bf16[128,4096]{1,0:T(8,128)(2,1)S(1)} %copy-done.4, bf16[128,4096]{1,0:T(8,128)(2,1)S(1)} %copy-done.8, bf16[128,4096]{1,0:T(8,128)(2,1)S(1)} %copy-done, bf16[128,4096]{1,0:T(8,128)(2,1)S(1)} %get-tuple-element.71.mate_k, ...), custom_call_target="tpu_custom_call" | custom-call | flops 1073741824 | bytes 8388608 | tf_op jit(solution)/shard_map/cond/branch_0_fun/here/pallas_call | solution.py:328
  17.7 3.2 %plan.4 = (s32[60]{0:T(128)S(1)}, s32[33]{0:T(128)S(1)}, s32[32]{0:T(128)S(1)}, s32[32]{0:T(128)S(1)}) custom-call(s32[4]{0:T(128)S(1)} %get-tuple-element.75.where, s32[16,128]{1,0:T(8,128)S(1)} %get-tuple-element.76.takes), custom_call_target="tpu_custom_call" | custom-call | flops 4294967296 | bytes 8388608 | tf_op jit(solution)/shard_map/cond/branch_0_fun/plan/pallas_call | solution.py:319
  21.0 8.2 %collective-permute-done.4.q_ref = bf16[128,4096]{1,0:T(8,128)(2,1)S(1)} collective-permute-done((bf16[128,4096]{1,0:T(8,128)(2,1)}, bf16[128,4096]{1,0:T(8,128)(2,1)S(1)}, u32[]{:S(2)}, u32[]{:S(2)}) %collective-permute-start.4) | collective-permute-done | bytes 1048608 | tf_op jit(solution)/shard_map/cond/branch_0_fun/ppermute | solution.py:302
  29.2 1.9 %far.7 = (bf16[9,128,128]{2,1,0:T(8,128)(2,1)S(1)}, f32[128,128]{1,0:T(8,128)S(1)}) custom-call(s32[32]{0:T(128)S(1)} %get-tuple-element.78.order, f32[128,128]{1,0:T(8,128)S(1)} %get-tuple-element.83.lse_ref, bf16[128,4096]{1,0:T(8,128)(2,1)S(1)} %collective-permute-done.4.q_ref, bf16[32,128,256]{2,1,0:T(8,128)(2,1)S(1)} %get-tuple-element.84.turned, ...), custom_call_target="tpu_custom_call" | custom-call | flops 1073741824 | bytes 8388608 | tf_op jit(solution)/shard_map/cond/branch_0_fun/far/pallas_call | solution.py:339
  31.1 1.3 %collective-permute-start.5 = (bf16[9,128,128]{2,1,0:T(8,128)(2,1)S(1)}, bf16[9,128,128]{2,1,0:T(8,128)(2,1)S(1)}, u32[]{:S(2)}, u32[]{:S(2)}) collective-permute-start(bf16[9,128,128]{2,1,0:T(8,128)(2,1)S(1)} %get-tuple-element.88), channel_id=1, source_target_pairs={{0,2},{1,3},{2,0},{3,1},{4,6},{5,7},{6,4},{7,5},{8,10},{9,11},{10,... | collective-permute-start | bytes 884744 | tf_op jit(solution)/shard_map/cond/branch_0_fun/ppermute | solution.py:354
  32.4 4.1 %far.8 = (bf16[7,128,128]{2,1,0:T(8,128)(2,1)S(1)}, f32[16,128,128]{2,1,0:T(8,128)S(1)}, f32[128,128]{1,0:T(8,128)S(1)}) custom-call(s32[32]{0:T(128)S(1)} %get-tuple-element.78.order, f32[128,128]{1,0:T(8,128)S(1)} %get-tuple-element.85.lse_ref, bf16[128,4096]{1,0:T(8,128)(2,1)S(1)} %collective-permute-done.4.q_ref, ...), custom_call_target="tpu_custom_call" | custom-call | flops 1073741824 | bytes 8388608 | tf_op jit(solution)/shard_map/cond/branch_0_fun/far/pallas_call | solution.py:339
  36.4 2.5 %collective-permute-done.5.rest_0_ = bf16[9,128,128]{2,1,0:T(8,128)(2,1)S(1)} collective-permute-done((bf16[9,128,128]{2,1,0:T(8,128)(2,1)S(1)}, bf16[9,128,128]{2,1,0:T(8,128)(2,1)S(1)}, u32[]{:S(2)}, u32[]{:S(2)}) %collective-permute-start.5) | collective-permute-done | bytes 294944 | tf_op jit(solution)/shard_map/cond/branch_0_fun/ppermute | solution.py:354
  39.0 1.7 %collective-permute-start.6 = (bf16[5,2,128,128]{3,2,1,0:T(8,128)(2,1)S(1)}, bf16[5,2,128,128]{3,2,1,0:T(8,128)(2,1)S(1)}, u32[]{:S(2)}, u32[]{:S(2)}) collective-permute-start(bf16[5,2,128,128]{3,2,1,0:T(8,128)(2,1)S(1)} %collective-permute-done.1.rest_0_), channel_id=1, source_target_pairs={{0,1},{1,0},{2,3},{3,2},{4,5},{5,4},{6,7},{7,6},{8,9},{9,8},{10,11... | collective-permute-start | bytes 983048 | tf_op jit(solution)/shard_map/cond/branch_0_fun/ppermute | solution.py:362
  40.7 0.4 collective-permute-start.8
  41.1 1.2 %collective-permute-start.10 = (bf16[7,128,128]{2,1,0:T(8,128)(2,1)S(1)}, bf16[7,128,128]{2,1,0:T(8,128)(2,1)S(1)}, u32[]{:S(2)}, u32[]{:S(2)}) collective-permute-start(bf16[7,128,128]{2,1,0:T(8,128)(2,1)S(1)} %get-tuple-element.98), channel_id=1, source_target_pairs={{0,2},{1,3},{2,0},{3,1},{4,6},{5,7},{6,4},{7,5},{8,10},{9,11},{10,... | collective-permute-start | bytes 688136 | tf_op jit(solution)/shard_map/cond/branch_0_fun/ppermute | solution.py:357
  42.8 3.5 %late.9 = (bf16[5,128,128]{2,1,0:T(8,128)(2,1)S(1)}, bf16[5,128,128]{2,1,0:T(8,128)(2,1)S(1)}, bf16[6,128,128]{2,1,0:T(8,128)(2,1)S(1)}, f32[32,128]{1,0:T(8,128)S(1)}) custom-call(s32[32]{0:T(128)S(1)} %get-tuple-element.78.order, s32[60]{0:T(128)S(1)} %get-tuple-element.79.pair, s32[33]{0:T(128)S(1)} %get-tuple-element.80.begin, ...), custom_call_target="tpu_custom_call" | custom-call | flops 1048576 | bytes 8388608 | tf_op jit(solution)/shard_map/cond/branch_0_fun/late/pallas_call | solution.py:365
  46.3 1.8 %collective-permute-start.13 = (bf16[6,128,128]{2,1,0:T(8,128)(2,1)S(1)}, bf16[6,128,128]{2,1,0:T(8,128)(2,1)S(1)}, u32[]{:S(2)}, u32[]{:S(2)}) collective-permute-start(bf16[6,128,128]{2,1,0:T(8,128)(2,1)S(1)} %get-tuple-element.101), channel_id=1, source_target_pairs={{0,2},{1,3},{2,0},{3,1},{4,6},{5,7},{6,4},{7,5},{8,10},{9,11},{10,... | collective-permute-start | bytes 589832 | tf_op jit(solution)/shard_map/cond/branch_0_fun/ppermute | solution.py:382
  48.2 1.4 %collective-permute-start.12 = (bf16[5,128,128]{2,1,0:T(8,128)(2,1)S(1)}, bf16[5,128,128]{2,1,0:T(8,128)(2,1)S(1)}, u32[]{:S(2)}, u32[]{:S(2)}) collective-permute-start(bf16[5,128,128]{2,1,0:T(8,128)(2,1)S(1)} %get-tuple-element.100), channel_id=1, source_target_pairs={{0,2},{1,3},{2,0},{3,1},{4,6},{5,7},{6,4},{7,5},{8,10},{9,11},{10,... | collective-permute-start | bytes 491528 | tf_op jit(solution)/shard_map/cond/branch_0_fun/ppermute | solution.py:382
  49.7 4.5 %late.8 = (f32[32,128,128]{2,1,0:T(8,128)S(1)}, f32[128,128]{1,0:T(8,128)S(1)}) custom-call(s32[32]{0:T(128)S(1)} %get-tuple-element.78.order, s32[60]{0:T(128)S(1)} %get-tuple-element.79.pair, s32[33]{0:T(128)S(1)} %get-tuple-element.80.begin, bf16[128,4096]{1,0:T(8,128)(2,1)S(1)} %copy-done.4, f32[32,128,128]{2,1,0:T(8,128)S(1)} %get-tuple-element.82.o_ref, ...), custom_call_target="tpu_custom_call" | custom-call | flops 1048576 | bytes 8388608 | tf_op jit(solution)/shard_map/cond/branch_0_fun/late/pallas_call | solution.py:365
  54.2 6.3 %collective-permute-done.9.lse_got = f32[32,128]{1,0:T(8,128)S(1)} collective-permute-done((f32[32,128]{1,0:T(8,128)S(1)}, f32[32,128]{1,0:T(8,128)S(1)}, u32[]{:S(2)}, u32[]{:S(2)}) %collective-permute-start.9) | collective-permute-done | bytes 16416 | tf_op jit(solution)/shard_map/cond/branch_0_fun/ppermute | solution.py:382
  60.5 2.2 %merge.4 = bf16[128,4096]{1,0:T(8,128)(2,1)} custom-call(s32[32]{0:T(128)S(1)} %get-tuple-element.77.far, f32[32,128,128]{2,1,0:T(8,128)S(1)} %get-tuple-element.92.mine, f32[128,128]{1,0:T(8,128)S(1)} %get-tuple-element.93.lse_here, f32[32,128]{1,0:T(8,128)S(1)} %collective-permute-done.9.lse_got, bf16[9,128,128]{2,1,0:T(8,128)(2,1)S(1)} %collective-permute-done.5.rest_0_, ...), custom_call_target="tpu_custom_call" | custom-call | flops 1048576 | bytes 8388608 | tf_op jit(solution)/shard_map/cond/branch_0_fun/merge/pallas_call | solution.py:385
  (23 shorter events, 1.1 us)
Async XLA Ops:
  0.0 2.9 %collective-permute-start.54 = (bf16[128,4096]{1,0:T(8,128)(2,1)}, bf16[128,4096]{1,0:T(8,128)(2,1)S(1)}, u32[]{:S(2)}, u32[]{:S(2)}) collective-permute-start(bf16[128,4096]{1,0:T(8,128)(2,1)} %param.10), channel_id=1, source_target_pairs={{0,1},{1,0},{2,3},{3,2},{4,5},{5,4},{6,7},{7,6},{8,9},{9,8},{10,11... | collective-permute-start | bytes 3145736 | tf_op jit(solution)/shard_map/ppermute | solution.py:405
  2.9 2.9 %collective-permute-start = (bf16[128,4096]{1,0:T(8,128)(2,1)}, bf16[128,4096]{1,0:T(8,128)(2,1)S(1)}, u32[]{:S(2)}, u32[]{:S(2)}) collective-permute-start(bf16[128,4096]{1,0:T(8,128)(2,1)} %get-tuple-element.221.v_ref), channel_id=1, source_target_pairs={{0,1},{1,0},{2,3},{3,2},{4,5},{5,4},{6,7},{7,6},{8,9},{9,8},{10,11... | collective-permute-start | bytes 3145736 | tf_op jit(solution)/shard_map/cond/branch_0_fun/ppermute | solution.py:301
  3.0 26.2 %collective-permute-start.4 = (bf16[128,4096]{1,0:T(8,128)(2,1)}, bf16[128,4096]{1,0:T(8,128)(2,1)S(1)}, u32[]{:S(2)}, u32[]{:S(2)}) collective-permute-start(bf16[128,4096]{1,0:T(8,128)(2,1)} %get-tuple-element.225.q_ref), channel_id=1, source_target_pairs={{0,2},{1,3},{2,0},{3,1},{4,6},{5,7},{6,4},{7,5},{8,10},{9,11},{10,... | collective-permute-start | bytes 3145736 | tf_op jit(solution)/shard_map/cond/branch_0_fun/ppermute | solution.py:302
  5.7 7.6 %copy-start = (bf16[128,4096]{1,0:T(8,128)(2,1)S(1)}, bf16[128,4096]{1,0:T(8,128)(2,1)}, u32[]{:S(2)}) copy-start(bf16[128,4096]{1,0:T(8,128)(2,1)} %get-tuple-element.221.v_ref) | copy-start | bytes 3145732 | tf_op jit(solution)/shard_map/cond
  5.7 7.6 %copy-start.4 = (bf16[128,4096]{1,0:T(8,128)(2,1)S(1)}, bf16[128,4096]{1,0:T(8,128)(2,1)}, u32[]{:S(2)}) copy-start(bf16[128,4096]{1,0:T(8,128)(2,1)} %get-tuple-element.225.q_ref) | copy-start | bytes 3145732 | tf_op jit(solution)/shard_map/cond
  5.7 7.6 %copy-start.8 = (bf16[128,4096]{1,0:T(8,128)(2,1)S(1)}, bf16[128,4096]{1,0:T(8,128)(2,1)}, u32[]{:S(2)}) copy-start(bf16[128,4096]{1,0:T(8,128)(2,1)} %get-tuple-element.69.k_ref) | copy-start | bytes 3145732 | tf_op jit(solution)/shard_map/cond
  7.5 31.4 %collective-permute-start.1 = (bf16[5,2,128,128]{3,2,1,0:T(8,128)(2,1)S(1)}, bf16[5,2,128,128]{3,2,1,0:T(8,128)(2,1)S(1)}, u32[]{:S(2)}, u32[]{:S(2)}) collective-permute-start(bf16[5,2,128,128]{3,2,1,0:T(8,128)(2,1)S(1)} %get-tuple-element.72), channel_id=1, source_target_pairs={{0,4},{1,5},{2,6},{3,7},{4,8},{5,9},{6,10},{7,11},{8,12},{9,13},{1... | collective-permute-start | bytes 983048 | tf_op jit(solution)/shard_map/cond/branch_0_fun/ppermute | solution.py:313
  10.0 29.0 %collective-permute-start.2 = (bf16[5,2,128,128]{3,2,1,0:T(8,128)(2,1)S(1)}, bf16[5,2,128,128]{3,2,1,0:T(8,128)(2,1)S(1)}, u32[]{:S(2)}, u32[]{:S(2)}) collective-permute-start(bf16[5,2,128,128]{3,2,1,0:T(8,128)(2,1)S(1)} %get-tuple-element.73), channel_id=1, source_target_pairs={{0,8},{1,9},{2,10},{3,11},{4,12},{5,13},{6,14},{7,15},{8,0},{9,1},... | collective-permute-start | bytes 983048 | tf_op jit(solution)/shard_map/cond/branch_0_fun/ppermute | solution.py:313
  12.3 26.7 %collective-permute-start.3 = (bf16[5,2,128,128]{3,2,1,0:T(8,128)(2,1)S(1)}, bf16[5,2,128,128]{3,2,1,0:T(8,128)(2,1)S(1)}, u32[]{:S(2)}, u32[]{:S(2)}) collective-permute-start(bf16[5,2,128,128]{3,2,1,0:T(8,128)(2,1)S(1)} %get-tuple-element.74), channel_id=1, source_target_pairs={{0,12},{1,13},{2,14},{3,15},{4,0},{5,1},{6,2},{7,3},{8,4},{9,5},{1... | collective-permute-start | bytes 983048 | tf_op jit(solution)/shard_map/cond/branch_0_fun/ppermute | solution.py:313
  31.1 7.9 %collective-permute-start.5 = (bf16[9,128,128]{2,1,0:T(8,128)(2,1)S(1)}, bf16[9,128,128]{2,1,0:T(8,128)(2,1)S(1)}, u32[]{:S(2)}, u32[]{:S(2)}) collective-permute-start(bf16[9,128,128]{2,1,0:T(8,128)(2,1)S(1)} %get-tuple-element.88), channel_id=1, source_target_pairs={{0,2},{1,3},{2,0},{3,1},{4,6},{5,7},{6,4},{7,5},{8,10},{9,11},{10,... | collective-permute-start | bytes 884744 | tf_op jit(solution)/shard_map/cond/branch_0_fun/ppermute | solution.py:354
  39.0 3.4 %collective-permute-start.6 = (bf16[5,2,128,128]{3,2,1,0:T(8,128)(2,1)S(1)}, bf16[5,2,128,128]{3,2,1,0:T(8,128)(2,1)S(1)}, u32[]{:S(2)}, u32[]{:S(2)}) collective-permute-start(bf16[5,2,128,128]{3,2,1,0:T(8,128)(2,1)S(1)} %collective-permute-done.1.rest_0_), channel_id=1, source_target_pairs={{0,1},{1,0},{2,3},{3,2},{4,5},{5,4},{6,7},{7,6},{8,9},{9,8},{10,11... | collective-permute-start | bytes 983048 | tf_op jit(solution)/shard_map/cond/branch_0_fun/ppermute | solution.py:362
  40.6 1.8 %collective-permute-start.7 = (bf16[5,2,128,128]{3,2,1,0:T(8,128)(2,1)S(1)}, bf16[5,2,128,128]{3,2,1,0:T(8,128)(2,1)S(1)}, u32[]{:S(2)}, u32[]{:S(2)}) collective-permute-start(bf16[5,2,128,128]{3,2,1,0:T(8,128)(2,1)S(1)} %collective-permute-done.2.rest_2_), channel_id=1, source_target_pairs={{0,1},{1,0},{2,3},{3,2},{4,5},{5,4},{6,7},{7,6},{8,9},{9,8},{10,11... | collective-permute-start | bytes 983048 | tf_op jit(solution)/shard_map/cond/branch_0_fun/ppermute | solution.py:362
  40.7 2.1 %collective-permute-start.8 = (bf16[5,2,128,128]{3,2,1,0:T(8,128)(2,1)S(1)}, bf16[5,2,128,128]{3,2,1,0:T(8,128)(2,1)S(1)}, u32[]{:S(2)}, u32[]{:S(2)}) collective-permute-start(bf16[5,2,128,128]{3,2,1,0:T(8,128)(2,1)S(1)} %collective-permute-done.3.rest_4_), channel_id=1, source_target_pairs={{0,1},{1,0},{2,3},{3,2},{4,5},{5,4},{6,7},{7,6},{8,9},{9,8},{10,11... | collective-permute-start | bytes 983048 | tf_op jit(solution)/shard_map/cond/branch_0_fun/ppermute | solution.py:362
  41.1 13.1 %collective-permute-start.10 = (bf16[7,128,128]{2,1,0:T(8,128)(2,1)S(1)}, bf16[7,128,128]{2,1,0:T(8,128)(2,1)S(1)}, u32[]{:S(2)}, u32[]{:S(2)}) collective-permute-start(bf16[7,128,128]{2,1,0:T(8,128)(2,1)S(1)} %get-tuple-element.98), channel_id=1, source_target_pairs={{0,2},{1,3},{2,0},{3,1},{4,6},{5,7},{6,4},{7,5},{8,10},{9,11},{10,... | collective-permute-start | bytes 688136 | tf_op jit(solution)/shard_map/cond/branch_0_fun/ppermute | solution.py:357
  46.3 14.2 %collective-permute-start.13 = (bf16[6,128,128]{2,1,0:T(8,128)(2,1)S(1)}, bf16[6,128,128]{2,1,0:T(8,128)(2,1)S(1)}, u32[]{:S(2)}, u32[]{:S(2)}) collective-permute-start(bf16[6,128,128]{2,1,0:T(8,128)(2,1)S(1)} %get-tuple-element.101), channel_id=1, source_target_pairs={{0,2},{1,3},{2,0},{3,1},{4,6},{5,7},{6,4},{7,5},{8,10},{9,11},{10,... | collective-permute-start | bytes 589832 | tf_op jit(solution)/shard_map/cond/branch_0_fun/ppermute | solution.py:382
  48.2 12.3 %collective-permute-start.11 = (bf16[5,128,128]{2,1,0:T(8,128)(2,1)S(1)}, bf16[5,128,128]{2,1,0:T(8,128)(2,1)S(1)}, u32[]{:S(2)}, u32[]{:S(2)}) collective-permute-start(bf16[5,128,128]{2,1,0:T(8,128)(2,1)S(1)} %get-tuple-element.99), channel_id=1, source_target_pairs={{0,2},{1,3},{2,0},{3,1},{4,6},{5,7},{6,4},{7,5},{8,10},{9,11},{10,... | collective-permute-start | bytes 491528 | tf_op jit(solution)/shard_map/cond/branch_0_fun/ppermute | solution.py:382
  48.2 12.3 %collective-permute-start.12 = (bf16[5,128,128]{2,1,0:T(8,128)(2,1)S(1)}, bf16[5,128,128]{2,1,0:T(8,128)(2,1)S(1)}, u32[]{:S(2)}, u32[]{:S(2)}) collective-permute-start(bf16[5,128,128]{2,1,0:T(8,128)(2,1)S(1)} %get-tuple-element.100), channel_id=1, source_target_pairs={{0,2},{1,3},{2,0},{3,1},{4,6},{5,7},{6,4},{7,5},{8,10},{9,11},{10,... | collective-permute-start | bytes 491528 | tf_op jit(solution)/shard_map/cond/branch_0_fun/ppermute | solution.py:382
  49.6 10.9 %collective-permute-start.9 = (f32[32,128]{1,0:T(8,128)S(1)}, f32[32,128]{1,0:T(8,128)S(1)}, u32[]{:S(2)}, u32[]{:S(2)}) collective-permute-start(f32[32,128]{1,0:T(8,128)S(1)} %get-tuple-element.96), channel_id=1, source_target_pairs={{0,2},{1,3},{2,0},{3,1},{4,6},{5,7},{6,4},{7,5},{8,10},{9,11},{10,... | collective-permute-start | bytes 49160 | tf_op jit(solution)/shard_map/cond/branch_0_fun/ppermute | solution.py:382
where the time goes:
time: 64.4 us; the launch traced here: 63.2 us
  Pallas kernels  27 us (42%)
  waiting for transfers between devices  18.3 us (28%)
  starting transfers between devices  16.7 us (26%)
  between operations  0.84 us (1%)
    ppermute x1, waiting for transfers between devices, exchange(): far_q = lax.ppermute(queries, 'seq', across)  8.23 us
    pallas_call x2, Pallas kernels, add_extras(): pl.pallas_call(functools.partial(late_kernel, len(boxes), early, by_head,...  8 us
    ppermute x1, waiting for transfers between devices, exchange(): lax.ppermute(lse_far, 'seq', across)  6.3 us
    pallas_call x2, Pallas kernels, attend_far(): pl.pallas_call(functools.partial(far_kernel, start), out_shape=[shape((n,...  5.94 us
    ppermute x3, starting transfers between devices, exchange(): lax.ppermute(packed[step - 1], 'seq', [(d, (d + OWN * step) % count) for...  5.86 us
    pallas_call x1, Pallas kernels, exchange(): pl.pallas_call(functools.partial(here_kernel, heads), out_shape=[shape((h...  4.33 us
    ppermute x3, starting transfers between devices, exchange(): lax.ppermute(x, 'seq', across)  3.27 us
    pallas_call x1, Pallas kernels, exchange(): pl.pallas_call(functools.partial(plan_kernel, heads, planes, room), out_s...  3.24 us
  transfers between devices with their start and end apart: 15, of which 6 were waited for; matrix products, arithmetic and copies ran while one was open for 0% of the time, Pallas kernels for 39%

commit v1 on v0

--- a/solution.py
+++ b/solution.py
@@ -12,7 +12,7 @@
 KTILE = 128
 GROUP = 4
 OWN = QTILE // KTILE
-SIZES = ((5, 16), (6, 18), (7, 20))
+SIZES = ((5, 14), (5, 16), (6, 18), (7, 20))
 MIB = 1 << 20
 SMEM = pl.BlockSpec(memory_space=pltpu.SMEM)
 VMEM = pl.BlockSpec(memory_space=pltpu.VMEM)
@@ -346,7 +346,7 @@
             name="far",
         )(order, lse, far_q, turned, values, mate_v)
 
-    second = min(early, thirds(late)[-1] + 1)
+    second = min(early, max(thirds(late)[-1] + 2, early - 8))
     parts = [n for n in (early - second, second) if n]
     lse_far, arrived = lse_here, []
     if early:

time: 64.4 us -> 63.8 us (level)
  waiting for transfers between devices: 18.3 us -> 15.7 us
  Pallas kernels: 27 us -> 29.1 us
    pallas_call x2, Pallas kernels: 8 us -> 9.74 us  [add_extras(): pl.pallas_call(functools.partial(late_kernel, len(boxes), early, by_head,...]
    ppermute x1, waiting for transfers between devices: 6.3 us -> 5.02 us  [exchange(): lax.ppermute(lse_far, 'seq', across)]
    ppermute x1, waiting for transfers between devices: 2.51 us -> 1.46 us  [exchange(): arrived = [lax.ppermute(sent, 'seq', across)]]
    ppermute x3, starting transfers between devices: 3.27 us -> 2.24 us  [exchange(): lax.ppermute(x, 'seq', across)]
    ppermute x1, starting transfers between devices: 0.08 us -> 0.75 us  [exchange(): lax.ppermute(lse_far, 'seq', across)]
  transfers between devices with their start and end apart: 15 -> 15, of which waited for: 6 -> 6; matrix products, arithmetic and copies ran while one was open for 0% -> 0% of each run, Pallas kernels for 39% -> 43%
where the time goes in v1:
time: 63.8 us; the launch traced here: 62.6 us
  Pallas kernels  29.1 us (46%)
  starting transfers between devices  16.2 us (25%)
  waiting for transfers between devices  15.7 us (25%)
  between operations  0.88 us (1%)
    pallas_call x2, Pallas kernels, add_extras(): pl.pallas_call(functools.partial(late_kernel, len(boxes), early, by_head,...  9.74 us
    ppermute x1, waiting for transfers between devices, exchange(): far_q = lax.ppermute(queries, 'seq', across)  7.96 us
    pallas_call x2, Pallas kernels, attend_far(): pl.pallas_call(functools.partial(far_kernel, start), out_shape=[shape((n,...  5.96 us
    ppermute x3, starting transfers between devices, exchange(): lax.ppermute(packed[step - 1], 'seq', [(d, (d + OWN * step) % count) for...  5.77 us
    ppermute x1, waiting for transfers between devices, exchange(): lax.ppermute(lse_far, 'seq', across)  5.02 us
    pallas_call x1, Pallas kernels, exchange(): pl.pallas_call(functools.partial(here_kernel, heads), out_shape=[shape((h...  4.33 us
    pallas_call x1, Pallas kernels, exchange(): pl.pallas_call(functools.partial(plan_kernel, heads, planes, room), out_s...  3.24 us
    ppermute x1, starting transfers between devices, exchange(): far_q = lax.ppermute(queries, 'seq', across)  2.58 us
  transfers between devices with their start and end apart: 15, of which 6 were waited for; matrix products, arithmetic and copies ran while one was open for 0% of the time, Pallas kernels for 43%

profile of v1, /device:TPU:1, one launch (start us, length us, event | category | flops | bytes accessed | tf_op | source)
XLA Modules:
  0.0 62.6 jit_solution(2624511800852069768)
XLA Ops:
  0.1 1.5 %lists.1 = (s32[40,128]{1,0:T(8,128)S(1)}, s32[16,128]{1,0:T(8,128)S(1)}, s32[1]{0:T(128)}) custom-call(s32[4]{0:T(128)S(1)} %pad_add_fusion.where, s32[32,32]{1,0:T(8,128)} %bitcast.9, s32[4,32]{1,0:T(4,128)} %bitcast.10), custom_call_target="tpu_custom_call" | custom-call | tf_op jit(solution)/shard_map/lists/pallas_call | solution.py:407
  2.9 59.5 %conditional.1 = (bf16[128,4096]{1,0:T(8,128)(2,1)}) conditional(s32[]{:T(128)} %bitcast.7, (bf16[128,4096]{1,0:T(8,128)(2,1)}, s32[4]{0:T(128)S(1)}, s32[40,128]{1,0:T(8,128)S(1)}, bf16[128,4096]{1,0:T(8,128)(2,1)}, bf16[128,4096]{1,0:T(8,128)(2,1)S(1)}, /*index=5*/s32[16,128]{1,0:T(8,128)S(1)}, ...), branch_computations={%region_0.0_spmd, %region_1.0_spmd, %region_2.0_spmd, %region_3.0_... | conditional | flops 11814305792 | bytes 184615584 | solution.py:420
  3.0 2.6 %collective-permute-start.4 = (bf16[128,4096]{1,0:T(8,128)(2,1)}, bf16[128,4096]{1,0:T(8,128)(2,1)S(1)}, u32[]{:S(2)}, u32[]{:S(2)}) collective-permute-start(bf16[128,4096]{1,0:T(8,128)(2,1)} %get-tuple-element.279.q_ref), channel_id=1, source_target_pairs={{0,2},{1,3},{2,0},{3,1},{4,6},{5,7},{6,4},{7,5},{8,10},{9,11},{10,... | collective-permute-start | bytes 3145736 | tf_op jit(solution)/shard_map/cond/branch_0_fun/ppermute | solution.py:302
  5.8 2.1 %pack.5 = (bf16[5,2,128,128]{3,2,1,0:T(8,128)(2,1)S(1)}, bf16[5,2,128,128]{3,2,1,0:T(8,128)(2,1)S(1)}, bf16[5,2,128,128]{3,2,1,0:T(8,128)(2,1)S(1)}) custom-call(s32[4]{0:T(128)S(1)} %get-tuple-element.90.where, s32[40,128]{1,0:T(8,128)S(1)} %get-tuple-element.82.sends, bf16[128,4096]{1,0:T(8,128)(2,1)} %get-tuple-element.84.k_ref, ...), custom_call_target="tpu_custom_call" | custom-call | flops 4294967296 | bytes 8388608 | tf_op jit(solution)/shard_map/cond/branch_0_fun/pack/pallas_call | solution.py:303
  7.9 2.1 %collective-permute-start.1 = (bf16[5,2,128,128]{3,2,1,0:T(8,128)(2,1)S(1)}, bf16[5,2,128,128]{3,2,1,0:T(8,128)(2,1)S(1)}, u32[]{:S(2)}, u32[]{:S(2)}) collective-permute-start(bf16[5,2,128,128]{3,2,1,0:T(8,128)(2,1)S(1)} %get-tuple-element.87), channel_id=1, source_target_pairs={{0,4},{1,5},{2,6},{3,7},{4,8},{5,9},{6,10},{7,11},{8,12},{9,13},{1... | collective-permute-start | bytes 983048 | tf_op jit(solution)/shard_map/cond/branch_0_fun/ppermute | solution.py:313
  10.0 2.4 %collective-permute-start.2 = (bf16[5,2,128,128]{3,2,1,0:T(8,128)(2,1)S(1)}, bf16[5,2,128,128]{3,2,1,0:T(8,128)(2,1)S(1)}, u32[]{:S(2)}, u32[]{:S(2)}) collective-permute-start(bf16[5,2,128,128]{3,2,1,0:T(8,128)(2,1)S(1)} %get-tuple-element.88), channel_id=1, source_target_pairs={{0,8},{1,9},{2,10},{3,11},{4,12},{5,13},{6,14},{7,15},{8,0},{9,1},... | collective-permute-start | bytes 983048 | tf_op jit(solution)/shard_map/cond/branch_0_fun/ppermute | solution.py:313
  12.4 1.3 %collective-permute-start.3 = (bf16[5,2,128,128]{3,2,1,0:T(8,128)(2,1)S(1)}, bf16[5,2,128,128]{3,2,1,0:T(8,128)(2,1)S(1)}, u32[]{:S(2)}, u32[]{:S(2)}) collective-permute-start(bf16[5,2,128,128]{3,2,1,0:T(8,128)(2,1)S(1)} %get-tuple-element.89), channel_id=1, source_target_pairs={{0,12},{1,13},{2,14},{3,15},{4,0},{5,1},{6,2},{7,3},{8,4},{9,5},{1... | collective-permute-start | bytes 983048 | tf_op jit(solution)/shard_map/cond/branch_0_fun/ppermute | solution.py:313
  13.7 4.3 %here.5 = (f32[32,128,128]{2,1,0:T(8,128)S(1)}, f32[128,128]{1,0:T(8,128)S(1)}, bf16[32,128,256]{2,1,0:T(8,128)(2,1)S(1)}) custom-call(bf16[128,4096]{1,0:T(8,128)(2,1)S(1)} %copy-done.5, bf16[128,4096]{1,0:T(8,128)(2,1)S(1)} %copy-done.10, bf16[128,4096]{1,0:T(8,128)(2,1)S(1)} %copy-done, bf16[128,4096]{1,0:T(8,128)(2,1)S(1)} %get-tuple-element.86.mate_k, ...), custom_call_target="tpu_custom_call" | custom-call | flops 1073741824 | bytes 8388608 | tf_op jit(solution)/shard_map/cond/branch_0_fun/here/pallas_call | solution.py:328
  18.0 3.2 %plan.5 = (s32[60]{0:T(128)S(1)}, s32[33]{0:T(128)S(1)}, s32[32]{0:T(128)S(1)}, s32[32]{0:T(128)S(1)}) custom-call(s32[4]{0:T(128)S(1)} %get-tuple-element.90.where, s32[16,128]{1,0:T(8,128)S(1)} %get-tuple-element.91.takes), custom_call_target="tpu_custom_call" | custom-call | flops 4294967296 | bytes 8388608 | tf_op jit(solution)/shard_map/cond/branch_0_fun/plan/pallas_call | solution.py:319
  21.2 8.0 %collective-permute-done.4.q_ref = bf16[128,4096]{1,0:T(8,128)(2,1)S(1)} collective-permute-done((bf16[128,4096]{1,0:T(8,128)(2,1)}, bf16[128,4096]{1,0:T(8,128)(2,1)S(1)}, u32[]{:S(2)}, u32[]{:S(2)}) %collective-permute-start.4) | collective-permute-done | bytes 1048608 | tf_op jit(solution)/shard_map/cond/branch_0_fun/ppermute | solution.py:302
  29.2 1.5 %far.9 = (bf16[8,128,128]{2,1,0:T(8,128)(2,1)S(1)}, f32[128,128]{1,0:T(8,128)S(1)}) custom-call(s32[32]{0:T(128)S(1)} %get-tuple-element.93.order, f32[128,128]{1,0:T(8,128)S(1)} %get-tuple-element.98.lse_ref, bf16[128,4096]{1,0:T(8,128)(2,1)S(1)} %collective-permute-done.4.q_ref, bf16[32,128,256]{2,1,0:T(8,128)(2,1)S(1)} %get-tuple-element.99.turned, ...), custom_call_target="tpu_custom_call" | custom-call | flops 1073741824 | bytes 8388608 | tf_op jit(solution)/shard_map/cond/branch_0_fun/far/pallas_call | solution.py:339
  30.7 1.3 %collective-permute-start.5 = (bf16[8,128,128]{2,1,0:T(8,128)(2,1)S(1)}, bf16[8,128,128]{2,1,0:T(8,128)(2,1)S(1)}, u32[]{:S(2)}, u32[]{:S(2)}) collective-permute-start(bf16[8,128,128]{2,1,0:T(8,128)(2,1)S(1)} %get-tuple-element.103), channel_id=1, source_target_pairs={{0,2},{1,3},{2,0},{3,1},{4,6},{5,7},{6,4},{7,5},{8,10},{9,11},{10,... | collective-permute-start | bytes 786440 | tf_op jit(solution)/shard_map/cond/branch_0_fun/ppermute | solution.py:354
  32.0 4.4 %far.10 = (bf16[10,128,128]{2,1,0:T(8,128)(2,1)S(1)}, f32[14,128,128]{2,1,0:T(8,128)S(1)}, f32[128,128]{1,0:T(8,128)S(1)}) custom-call(s32[32]{0:T(128)S(1)} %get-tuple-element.93.order, f32[128,128]{1,0:T(8,128)S(1)} %get-tuple-element.100.lse_ref, bf16[128,4096]{1,0:T(8,128)(2,1)S(1)} %collective-permute-done.4.q_ref, ...), custom_call_target="tpu_custom_call" | custom-call | flops 1073741824 | bytes 8388608 | tf_op jit(solution)/shard_map/cond/branch_0_fun/far/pallas_call | solution.py:339
  36.5 1.5 %collective-permute-done.5.rest_0_ = bf16[8,128,128]{2,1,0:T(8,128)(2,1)S(1)} collective-permute-done((bf16[8,128,128]{2,1,0:T(8,128)(2,1)S(1)}, bf16[8,128,128]{2,1,0:T(8,128)(2,1)S(1)}, u32[]{:S(2)}, u32[]{:S(2)}) %collective-permute-start.5) | collective-permute-done | bytes 262176 | tf_op jit(solution)/shard_map/cond/branch_0_fun/ppermute | solution.py:354
  37.9 1.7 %collective-permute-start.6 = (bf16[5,2,128,128]{3,2,1,0:T(8,128)(2,1)S(1)}, bf16[5,2,128,128]{3,2,1,0:T(8,128)(2,1)S(1)}, u32[]{:S(2)}, u32[]{:S(2)}) collective-permute-start(bf16[5,2,128,128]{3,2,1,0:T(8,128)(2,1)S(1)} %collective-permute-done.1.rest_0_), channel_id=1, source_target_pairs={{0,1},{1,0},{2,3},{3,2},{4,5},{5,4},{6,7},{7,6},{8,9},{9,8},{10,11... | collective-permute-start | bytes 983048 | tf_op jit(solution)/shard_map/cond/branch_0_fun/ppermute | solution.py:362
  40.1 1.2 %collective-permute-start.10 = (bf16[10,128,128]{2,1,0:T(8,128)(2,1)S(1)}, bf16[10,128,128]{2,1,0:T(8,128)(2,1)S(1)}, u32[]{:S(2)}, u32[]{:S(2)}) collective-permute-start(bf16[10,128,128]{2,1,0:T(8,128)(2,1)S(1)} %get-tuple-element.113), channel_id=1, source_target_pairs={{0,2},{1,3},{2,0},{3,1},{4,6},{5,7},{6,4},{7,5},{8,10},{9,11},{10,... | collective-permute-start | bytes 983048 | tf_op jit(solution)/shard_map/cond/branch_0_fun/ppermute | solution.py:357
  41.8 4.3 %late.11 = (bf16[4,128,128]{2,1,0:T(8,128)(2,1)S(1)}, bf16[4,128,128]{2,1,0:T(8,128)(2,1)S(1)}, bf16[6,128,128]{2,1,0:T(8,128)(2,1)S(1)}, f32[32,128]{1,0:T(8,128)S(1)}) custom-call(s32[32]{0:T(128)S(1)} %get-tuple-element.93.order, s32[60]{0:T(128)S(1)} %get-tuple-element.94.pair, s32[33]{0:T(128)S(1)} %get-tuple-element.95.begin, ...), custom_call_target="tpu_custom_call" | custom-call | flops 1048576 | bytes 8388608 | tf_op jit(solution)/shard_map/cond/branch_0_fun/late/pallas_call | solution.py:365
  46.1 0.8 %collective-permute-start.13 = (bf16[6,128,128]{2,1,0:T(8,128)(2,1)S(1)}, bf16[6,128,128]{2,1,0:T(8,128)(2,1)S(1)}, u32[]{:S(2)}, u32[]{:S(2)}) collective-permute-start(bf16[6,128,128]{2,1,0:T(8,128)(2,1)S(1)} %get-tuple-element.116), channel_id=1, source_target_pairs={{0,2},{1,3},{2,0},{3,1},{4,6},{5,7},{6,4},{7,5},{8,10},{9,11},{10,... | collective-permute-start | bytes 589832 | tf_op jit(solution)/shard_map/cond/branch_0_fun/ppermute | solution.py:382
  46.9 0.8 %collective-permute-start.11 = (bf16[4,128,128]{2,1,0:T(8,128)(2,1)S(1)}, bf16[4,128,128]{2,1,0:T(8,128)(2,1)S(1)}, u32[]{:S(2)}, u32[]{:S(2)}) collective-permute-start(bf16[4,128,128]{2,1,0:T(8,128)(2,1)S(1)} %get-tuple-element.114), channel_id=1, source_target_pairs={{0,2},{1,3},{2,0},{3,1},{4,6},{5,7},{6,4},{7,5},{8,10},{9,11},{10,... | collective-permute-start | bytes 393224 | tf_op jit(solution)/shard_map/cond/branch_0_fun/ppermute | solution.py:382
  47.6 0.7 %collective-permute-start.12 = (bf16[4,128,128]{2,1,0:T(8,128)(2,1)S(1)}, bf16[4,128,128]{2,1,0:T(8,128)(2,1)S(1)}, u32[]{:S(2)}, u32[]{:S(2)}) collective-permute-start(bf16[4,128,128]{2,1,0:T(8,128)(2,1)S(1)} %get-tuple-element.115), channel_id=1, source_target_pairs={{0,2},{1,3},{2,0},{3,1},{4,6},{5,7},{6,4},{7,5},{8,10},{9,11},{10,... | collective-permute-start | bytes 393224 | tf_op jit(solution)/shard_map/cond/branch_0_fun/ppermute | solution.py:382
  48.4 0.8 %collective-permute-start.9 = (f32[32,128]{1,0:T(8,128)S(1)}, f32[32,128]{1,0:T(8,128)S(1)}, u32[]{:S(2)}, u32[]{:S(2)}) collective-permute-start(f32[32,128]{1,0:T(8,128)S(1)} %get-tuple-element.111), channel_id=1, source_target_pairs={{0,2},{1,3},{2,0},{3,1},{4,6},{5,7},{6,4},{7,5},{8,10},{9,11},{10,... | collective-permute-start | bytes 49160 | tf_op jit(solution)/shard_map/cond/branch_0_fun/ppermute | solution.py:382
  49.1 5.4 %late.10 = (f32[32,128,128]{2,1,0:T(8,128)S(1)}, f32[128,128]{1,0:T(8,128)S(1)}) custom-call(s32[32]{0:T(128)S(1)} %get-tuple-element.93.order, s32[60]{0:T(128)S(1)} %get-tuple-element.94.pair, s32[33]{0:T(128)S(1)} %get-tuple-element.95.begin, bf16[128,4096]{1,0:T(8,128)(2,1)S(1)} %copy-done.5, f32[32,128,128]{2,1,0:T(8,128)S(1)} %get-tuple-element.97.o_ref, ...), custom_call_target="tpu_custom_call" | custom-call | flops 1048576 | bytes 8388608 | tf_op jit(solution)/shard_map/cond/branch_0_fun/late/pallas_call | solution.py:365
  54.5 5.0 %collective-permute-done.9.lse_got = f32[32,128]{1,0:T(8,128)S(1)} collective-permute-done((f32[32,128]{1,0:T(8,128)S(1)}, f32[32,128]{1,0:T(8,128)S(1)}, u32[]{:S(2)}, u32[]{:S(2)}) %collective-permute-start.9) | collective-permute-done | bytes 16416 | tf_op jit(solution)/shard_map/cond/branch_0_fun/ppermute | solution.py:382
  59.6 2.2 %merge.5 = bf16[128,4096]{1,0:T(8,128)(2,1)} custom-call(s32[32]{0:T(128)S(1)} %get-tuple-element.92.far, f32[32,128,128]{2,1,0:T(8,128)S(1)} %get-tuple-element.107.mine, f32[128,128]{1,0:T(8,128)S(1)} %get-tuple-element.108.lse_here, f32[32,128]{1,0:T(8,128)S(1)} %collective-permute-done.9.lse_got, ...), custom_call_target="tpu_custom_call" | custom-call | flops 1048576 | bytes 8388608 | tf_op jit(solution)/shard_map/cond/branch_0_fun/merge/pallas_call | solution.py:385
  (23 shorter events, 2.0 us)
Async XLA Ops:
  0.0 2.9 %collective-permute-start.68 = (bf16[128,4096]{1,0:T(8,128)(2,1)}, bf16[128,4096]{1,0:T(8,128)(2,1)S(1)}, u32[]{:S(2)}, u32[]{:S(2)}) collective-permute-start(bf16[128,4096]{1,0:T(8,128)(2,1)} %param.11), channel_id=1, source_target_pairs={{0,1},{1,0},{2,3},{3,2},{4,5},{5,4},{6,7},{7,6},{8,9},{9,8},{10,11... | collective-permute-start | bytes 3145736 | tf_op jit(solution)/shard_map/ppermute | solution.py:405
  2.9 2.9 %collective-permute-start = (bf16[128,4096]{1,0:T(8,128)(2,1)}, bf16[128,4096]{1,0:T(8,128)(2,1)S(1)}, u32[]{:S(2)}, u32[]{:S(2)}) collective-permute-start(bf16[128,4096]{1,0:T(8,128)(2,1)} %get-tuple-element.274.v_ref), channel_id=1, source_target_pairs={{0,1},{1,0},{2,3},{3,2},{4,5},{5,4},{6,7},{7,6},{8,9},{9,8},{10,11... | collective-permute-start | bytes 3145736 | tf_op jit(solution)/shard_map/cond/branch_0_fun/ppermute | solution.py:301
  3.0 26.2 %collective-permute-start.4 = (bf16[128,4096]{1,0:T(8,128)(2,1)}, bf16[128,4096]{1,0:T(8,128)(2,1)S(1)}, u32[]{:S(2)}, u32[]{:S(2)}) collective-permute-start(bf16[128,4096]{1,0:T(8,128)(2,1)} %get-tuple-element.279.q_ref), channel_id=1, source_target_pairs={{0,2},{1,3},{2,0},{3,1},{4,6},{5,7},{6,4},{7,5},{8,10},{9,11},{10,... | collective-permute-start | bytes 3145736 | tf_op jit(solution)/shard_map/cond/branch_0_fun/ppermute | solution.py:302
  5.7 7.9 %copy-start = (bf16[128,4096]{1,0:T(8,128)(2,1)S(1)}, bf16[128,4096]{1,0:T(8,128)(2,1)}, u32[]{:S(2)}) copy-start(bf16[128,4096]{1,0:T(8,128)(2,1)} %get-tuple-element.274.v_ref) | copy-start | bytes 3145732 | tf_op jit(solution)/shard_map/cond
  5.7 7.9 %copy-start.5 = (bf16[128,4096]{1,0:T(8,128)(2,1)S(1)}, bf16[128,4096]{1,0:T(8,128)(2,1)}, u32[]{:S(2)}) copy-start(bf16[128,4096]{1,0:T(8,128)(2,1)} %get-tuple-element.279.q_ref) | copy-start | bytes 3145732 | tf_op jit(solution)/shard_map/cond
  5.7 7.9 %copy-start.10 = (bf16[128,4096]{1,0:T(8,128)(2,1)S(1)}, bf16[128,4096]{1,0:T(8,128)(2,1)}, u32[]{:S(2)}) copy-start(bf16[128,4096]{1,0:T(8,128)(2,1)} %get-tuple-element.84.k_ref) | copy-start | bytes 3145732 | tf_op jit(solution)/shard_map/cond
  7.9 30.0 %collective-permute-start.1 = (bf16[5,2,128,128]{3,2,1,0:T(8,128)(2,1)S(1)}, bf16[5,2,128,128]{3,2,1,0:T(8,128)(2,1)S(1)}, u32[]{:S(2)}, u32[]{:S(2)}) collective-permute-start(bf16[5,2,128,128]{3,2,1,0:T(8,128)(2,1)S(1)} %get-tuple-element.87), channel_id=1, source_target_pairs={{0,4},{1,5},{2,6},{3,7},{4,8},{5,9},{6,10},{7,11},{8,12},{9,13},{1... | collective-permute-start | bytes 983048 | tf_op jit(solution)/shard_map/cond/branch_0_fun/ppermute | solution.py:313
  10.0 27.9 %collective-permute-start.2 = (bf16[5,2,128,128]{3,2,1,0:T(8,128)(2,1)S(1)}, bf16[5,2,128,128]{3,2,1,0:T(8,128)(2,1)S(1)}, u32[]{:S(2)}, u32[]{:S(2)}) collective-permute-start(bf16[5,2,128,128]{3,2,1,0:T(8,128)(2,1)S(1)} %get-tuple-element.88), channel_id=1, source_target_pairs={{0,8},{1,9},{2,10},{3,11},{4,12},{5,13},{6,14},{7,15},{8,0},{9,1},... | collective-permute-start | bytes 983048 | tf_op jit(solution)/shard_map/cond/branch_0_fun/ppermute | solution.py:313
  12.4 25.5 %collective-permute-start.3 = (bf16[5,2,128,128]{3,2,1,0:T(8,128)(2,1)S(1)}, bf16[5,2,128,128]{3,2,1,0:T(8,128)(2,1)S(1)}, u32[]{:S(2)}, u32[]{:S(2)}) collective-permute-start(bf16[5,2,128,128]{3,2,1,0:T(8,128)(2,1)S(1)} %get-tuple-element.89), channel_id=1, source_target_pairs={{0,12},{1,13},{2,14},{3,15},{4,0},{5,1},{6,2},{7,3},{8,4},{9,5},{1... | collective-permute-start | bytes 983048 | tf_op jit(solution)/shard_map/cond/branch_0_fun/ppermute | solution.py:313
  30.7 7.2 %collective-permute-start.5 = (bf16[8,128,128]{2,1,0:T(8,128)(2,1)S(1)}, bf16[8,128,128]{2,1,0:T(8,128)(2,1)S(1)}, u32[]{:S(2)}, u32[]{:S(2)}) collective-permute-start(bf16[8,128,128]{2,1,0:T(8,128)(2,1)S(1)} %get-tuple-element.103), channel_id=1, source_target_pairs={{0,2},{1,3},{2,0},{3,1},{4,6},{5,7},{6,4},{7,5},{8,10},{9,11},{10,... | collective-permute-start | bytes 786440 | tf_op jit(solution)/shard_map/cond/branch_0_fun/ppermute | solution.py:354
  37.9 3.4 %collective-permute-start.6 = (bf16[5,2,128,128]{3,2,1,0:T(8,128)(2,1)S(1)}, bf16[5,2,128,128]{3,2,1,0:T(8,128)(2,1)S(1)}, u32[]{:S(2)}, u32[]{:S(2)}) collective-permute-start(bf16[5,2,128,128]{3,2,1,0:T(8,128)(2,1)S(1)} %collective-permute-done.1.rest_0_), channel_id=1, source_target_pairs={{0,1},{1,0},{2,3},{3,2},{4,5},{5,4},{6,7},{7,6},{8,9},{9,8},{10,11... | collective-permute-start | bytes 983048 | tf_op jit(solution)/shard_map/cond/branch_0_fun/ppermute | solution.py:362
  39.6 1.8 %collective-permute-start.7 = (bf16[5,2,128,128]{3,2,1,0:T(8,128)(2,1)S(1)}, bf16[5,2,128,128]{3,2,1,0:T(8,128)(2,1)S(1)}, u32[]{:S(2)}, u32[]{:S(2)}) collective-permute-start(bf16[5,2,128,128]{3,2,1,0:T(8,128)(2,1)S(1)} %collective-permute-done.2.rest_2_), channel_id=1, source_target_pairs={{0,1},{1,0},{2,3},{3,2},{4,5},{5,4},{6,7},{7,6},{8,9},{9,8},{10,11... | collective-permute-start | bytes 983048 | tf_op jit(solution)/shard_map/cond/branch_0_fun/ppermute | solution.py:362
  39.7 2.1 %collective-permute-start.8 = (bf16[5,2,128,128]{3,2,1,0:T(8,128)(2,1)S(1)}, bf16[5,2,128,128]{3,2,1,0:T(8,128)(2,1)S(1)}, u32[]{:S(2)}, u32[]{:S(2)}) collective-permute-start(bf16[5,2,128,128]{3,2,1,0:T(8,128)(2,1)S(1)} %collective-permute-done.3.rest_4_), channel_id=1, source_target_pairs={{0,1},{1,0},{2,3},{3,2},{4,5},{5,4},{6,7},{7,6},{8,9},{9,8},{10,11... | collective-permute-start | bytes 983048 | tf_op jit(solution)/shard_map/cond/branch_0_fun/ppermute | solution.py:362
  40.1 14.4 %collective-permute-start.10 = (bf16[10,128,128]{2,1,0:T(8,128)(2,1)S(1)}, bf16[10,128,128]{2,1,0:T(8,128)(2,1)S(1)}, u32[]{:S(2)}, u32[]{:S(2)}) collective-permute-start(bf16[10,128,128]{2,1,0:T(8,128)(2,1)S(1)} %get-tuple-element.113), channel_id=1, source_target_pairs={{0,2},{1,3},{2,0},{3,1},{4,6},{5,7},{6,4},{7,5},{8,10},{9,11},{10,... | collective-permute-start | bytes 983048 | tf_op jit(solution)/shard_map/cond/branch_0_fun/ppermute | solution.py:357
  46.1 13.5 %collective-permute-start.13 = (bf16[6,128,128]{2,1,0:T(8,128)(2,1)S(1)}, bf16[6,128,128]{2,1,0:T(8,128)(2,1)S(1)}, u32[]{:S(2)}, u32[]{:S(2)}) collective-permute-start(bf16[6,128,128]{2,1,0:T(8,128)(2,1)S(1)} %get-tuple-element.116), channel_id=1, source_target_pairs={{0,2},{1,3},{2,0},{3,1},{4,6},{5,7},{6,4},{7,5},{8,10},{9,11},{10,... | collective-permute-start | bytes 589832 | tf_op jit(solution)/shard_map/cond/branch_0_fun/ppermute | solution.py:382
  46.9 12.7 %collective-permute-start.11 = (bf16[4,128,128]{2,1,0:T(8,128)(2,1)S(1)}, bf16[4,128,128]{2,1,0:T(8,128)(2,1)S(1)}, u32[]{:S(2)}, u32[]{:S(2)}) collective-permute-start(bf16[4,128,128]{2,1,0:T(8,128)(2,1)S(1)} %get-tuple-element.114), channel_id=1, source_target_pairs={{0,2},{1,3},{2,0},{3,1},{4,6},{5,7},{6,4},{7,5},{8,10},{9,11},{10,... | collective-permute-start | bytes 393224 | tf_op jit(solution)/shard_map/cond/branch_0_fun/ppermute | solution.py:382
  47.6 11.9 %collective-permute-start.12 = (bf16[4,128,128]{2,1,0:T(8,128)(2,1)S(1)}, bf16[4,128,128]{2,1,0:T(8,128)(2,1)S(1)}, u32[]{:S(2)}, u32[]{:S(2)}) collective-permute-start(bf16[4,128,128]{2,1,0:T(8,128)(2,1)S(1)} %get-tuple-element.115), channel_id=1, source_target_pairs={{0,2},{1,3},{2,0},{3,1},{4,6},{5,7},{6,4},{7,5},{8,10},{9,11},{10,... | collective-permute-start | bytes 393224 | tf_op jit(solution)/shard_map/cond/branch_0_fun/ppermute | solution.py:382
  48.4 11.2 %collective-permute-start.9 = (f32[32,128]{1,0:T(8,128)S(1)}, f32[32,128]{1,0:T(8,128)S(1)}, u32[]{:S(2)}, u32[]{:S(2)}) collective-permute-start(f32[32,128]{1,0:T(8,128)S(1)} %get-tuple-element.111), channel_id=1, source_target_pairs={{0,2},{1,3},{2,0},{3,1},{4,6},{5,7},{6,4},{7,5},{8,10},{9,11},{10,... | collective-permute-start | bytes 49160 | tf_op jit(solution)/shard_map/cond/branch_0_fun/ppermute | solution.py:382
